TPU v7x, 128 devices: a whole 4x4x4 slice. The times are simulated.
128 devices in a mesh: car: 8 (over z_hi, x), dom: 16 (over y, z_lo, core).
Axes of the slice: x: 4, y: 4, z: 4 (z_hi: 2, z_lo: 2; z = z_hi * 2 + z_lo), core: 2. Of those that a mesh axis runs over, the one named last changes fastest.
Arguments:
- points: bfloat16 [131072, 768], P(('car', 'dom')), parts along dimension 0, may hold values from -6 to 6
- norm_gain: float32 [768], replicated, may hold values from 0.25 to 1.75
- w_qkv: bfloat16 [768, 2304], replicated, may hold values from -0.12629537 to 0.12629537
- w_out: bfloat16 [768, 768], replicated, may hold values from -0.75 to 0.75
- w_cross_q: bfloat16 [768, 768], replicated, may hold values from -0.12629537 to 0.12629537
- w_cross_kv: bfloat16 [768, 1536], replicated, may hold values from -0.12629537 to 0.12629537
- w_cross_out: bfloat16 [768, 768], replicated, may hold values from -0.75 to 0.75
- live_blocks: int32 [128], P(('car', 'dom')), parts along dimension 0, may hold values from 4 to 8, as said below
- send_blocks: int32 [512], P(('car', 'dom')), parts along dimension 0, may hold values from 0 to 7, as said below
- neighbours: int32 [1024, 8], P(('car', 'dom')), parts along dimension 0, may hold values from 0 to 11, as said below
- neighbour_count: int32 [1024], P(('car', 'dom')), parts along dimension 0, may hold values from 2 to 8
- anchor_index: int32 [32768], P(('car', 'dom')), parts along dimension 0, may hold values from 0 to 1023, as said below
Outputs:
- mixed: bfloat16 [131072, 768], P(('car', 'dom')), parts along dimension 0
There are 8 independent parts, one for each index of `car`. A program takes and returns all parts, laid end to end along the dimension named above; an argument that names none is the same for every part. Nothing has to cross between parts.
Inputs may be any that keep to these rules, and one draw needn't show every extreme that they name: `live_blocks`: some partition of every car has all 8 blocks live. `send_blocks`: the 2 blocks of each list are distinct live blocks of the sending partition. `neighbours`: slot 0 of every block is the block itself; the first partition of a car names no block of a previous one and the last none of a next one; counted slots of a live block name live blocks. `anchor_index`: anchors lie in live blocks of their partition.
All inputs are finite; a program needn't handle non-finite values.
Results may differ from a plain program's by a relative error of at most 0.0086.
Values may be sent and summed in bfloat16 or wider, within the bound.
No kernel may reach another device: no remote copies, remote signals or barrier semaphores. Data moves between devices by JAX's collectives and lax.ppermute only.
A program may use at most 256 MiB of HBM per device.

v0:
```python
import functools

import jax
import jax.numpy as jnp
from jax import lax
from jax.experimental import pallas as pl
from jax.experimental.pallas import tpu as pltpu
from jax.sharding import PartitionSpec as P

HEADS = 12
BLK = 128
HB = 2
PAIR = 128
HALF = 64
CHUNK = 256
SCALE = HALF**-0.5 * 1.4426950408889634
LIMIT = 32 * 2**20
WIDE = 61 * 2**20
NEG = -1e30
F32 = jnp.float32
BF16 = jnp.bfloat16


def params(limit=LIMIT):
    return pltpu.CompilerParams(vmem_limit_bytes=limit)


def cost(flops, nbytes, trans=0):
    return pl.CostEstimate(flops=int(flops), bytes_accessed=int(nbytes), transcendentals=int(trans))


def struct(rows, cols, dtype=BF16):
    return jax.ShapeDtypeStruct((rows, cols), dtype)


def whole(array):
    return pl.BlockSpec(array.shape, lambda *_: (0,) * array.ndim)


def mm(a, b):
    return jnp.dot(a, b, preferred_element_type=F32)


def mm_t(a, b):
    return lax.dot_general(a, b, (((1,), (1,)), ((), ())), preferred_element_type=F32)


def normed_rows(rows, gain):
    floats = rows.astype(F32)
    factor = lax.rsqrt(jnp.mean(floats * floats, axis=-1, keepdims=True) + 1e-06)
    return (floats * factor * gain).astype(BF16)


def pick_kernel(send_ref, index_ref, source_ref, anchor_ref, prev_ref, next_ref, points_ref, sem):
    copy = pltpu.make_async_copy(source_ref, points_ref, sem)
    copy.start()
    rows = points_ref.shape[0]
    anchors = index_ref.shape[1]
    slot = lax.broadcasted_iota(jnp.int32, (rows, anchors), 0)
    chosen = jnp.where(slot == index_ref[...], 1.0, 0.0).astype(BF16)
    copy.wait()
    anchor_ref[...] = lax.dot_general(
        chosen, points_ref[...], (((0,), (0,)), ((), ())), preferred_element_type=F32
    ).astype(BF16)
    for place in range(HB):
        for base, out_ref in ((0, prev_ref), (HB, next_ref)):
            start = pl.multiple_of(send_ref[base + place] * BLK, BLK)
            out_ref[place * BLK : (place + 1) * BLK, :] = points_ref[pl.ds(start, BLK), :]


def pick(points, send_blocks, anchor_index):
    rows, width = points.shape
    anchors = anchor_index.shape[0]
    index = anchor_index.reshape(1, anchors)
    own = struct(anchors, width)
    side = struct(HB * BLK, width)
    return pl.pallas_call(
        pick_kernel,
        out_shape=(own, side, side),
        in_specs=[
            pl.BlockSpec(memory_space=pltpu.SMEM),
            pl.BlockSpec(memory_space=pltpu.VMEM),
            pl.BlockSpec(memory_space=pltpu.HBM),
        ],
        scratch_shapes=[pltpu.VMEM((rows, width), BF16), pltpu.SemaphoreType.DMA],
        compiler_params=params(WIDE),
        cost_estimate=cost(2 * anchors * rows * width, 4 * rows * width),
    )(send_blocks, index, points)


def project_kernel(points_ref, gain_ref, wqkv_ref, wcq_ref, out_ref, normed_ref):
    step = pl.program_id(0)
    rows = points_ref.shape[0]
    tile = rows // 4

    @pl.when(step == 0)
    def _():
        for at in range(0, rows, tile):
            normed = normed_rows(points_ref[at : at + tile, :], gain_ref[...])
            normed_ref[at : at + tile, :] = normed
            out_ref[at : at + tile, :] = (mm(normed, wqkv_ref[...]) * SCALE).astype(BF16)

    @pl.when((step == 1) | (step == 2))
    def _():
        out_ref[...] = mm(normed_ref[...], wqkv_ref[...]).astype(BF16)

    @pl.when(step == 3)
    def _():
        out_ref[...] = (mm(normed_ref[...], wcq_ref[...]) * SCALE).astype(BF16)


def project(points, gain, w_qkv, w_cross_q):
    rows, width = points.shape
    return pl.pallas_call(
        project_kernel,
        out_shape=struct(rows, 4 * width),
        grid=(4,),
        in_specs=[
            whole(points),
            whole(gain),
            pl.BlockSpec((width, width), lambda i: (0, jnp.minimum(i, 2))),
            whole(w_cross_q),
        ],
        out_specs=pl.BlockSpec((rows, width), lambda i: (0, i)),
        scratch_shapes=[pltpu.VMEM((rows, width), BF16)],
        compiler_params=params(),
        cost_estimate=cost(2 * rows * width * 4 * width, 20 * rows * width),
    )(points, gain, w_qkv, w_cross_q)


def split_heads(rows):
    lane = lax.broadcasted_iota(jnp.int32, rows.shape, 1)
    zero = jnp.zeros_like(rows)
    return jnp.concatenate(
        [jnp.where(lane < HALF, rows, zero), jnp.where(lane >= HALF, rows, zero)], axis=0
    )


def join_heads(both):
    count = both.shape[0] // 2
    lane = lax.broadcasted_iota(jnp.int32, (count, PAIR), 1)
    return jnp.where(lane < HALF, both[:count], both[count:])


def weigh(weights, values):
    ones = jnp.ones((values.shape[0], PAIR), BF16)
    return mm(weights.astype(BF16), jnp.concatenate([values, ones], axis=1))


def block_kernel(
    ids_ref,
    count_ref,
    live_ref,
    queries_ref,
    projected_ref,
    low_ref,
    high_ref,
    gain_ref,
    wk_ref,
    wv_ref,
    out_ref,
    table_ref,
    sems,
):
    block = pl.program_id(0)
    slots = ids_ref.shape[1]
    rows = projected_ref.shape[0]
    side, width = low_ref.shape

    @pl.when(block == 0)
    def _():
        copies = [
            pltpu.make_async_copy(
                projected_ref.at[:, (1 + n) * width : (2 + n) * width],
                table_ref.at[n, :rows],
                sems.at[n],
            )
            for n in range(2)
        ]
        for copy in copies:
            copy.start()
        for place, ref in enumerate((low_ref, high_ref)):
            normed = normed_rows(ref[...], gain_ref[...])
            at = rows + place * side
            table_ref[0, at : at + side, :] = mm(normed, wk_ref[...]).astype(BF16)
            table_ref[1, at : at + side, :] = mm(normed, wv_ref[...]).astype(BF16)
        for copy in copies:
            copy.wait()

    count = count_ref[block]
    pairs = jnp.where(block < live_ref[0], (count + 1) // 2, 0)

    @pl.when(pairs == 0)
    def _():
        out_ref[...] = jnp.zeros_like(out_ref)

    for used in range(1, slots // 2 + 1):

        @pl.when(pairs == used)
        def _(used=used):
            starts = [pl.multiple_of(ids_ref[block, n] * BLK, BLK) for n in range(2 * used)]
            dropped = jnp.where(count == 2 * used, 0.0, NEG)

            def rows_of(which, part, at):
                return jnp.concatenate(
                    [
                        table_ref[which, pl.ds(start, BLK), at : at + PAIR]
                        for start in starts[2 * part : 2 * part + 2]
                    ],
                    axis=0,
                )

            for at in range(0, width, PAIR):
                query = split_heads(queries_ref[:, at : at + PAIR])
                scores = [mm_t(query, rows_of(0, part, at)) for part in range(used)]
                last = scores[-1]
                scores[-1] = jnp.concatenate([last[:, :BLK], last[:, BLK:] + dropped], axis=1)
                top = functools.reduce(jnp.maximum, scores)
                top = jnp.max(top, axis=1, keepdims=True)
                total = sum(
                    weigh(jnp.exp2(scores[part] - top), rows_of(1, part, at))
                    for part in range(used)
                )
                out_ref[:, at : at + PAIR] = join_heads(total[:, :PAIR] / total[:, PAIR:]).astype(
                    BF16
                )


def block_attention(projected, low, high, gain, w_qkv, ids, counts, live):
    rows = projected.shape[0]
    width = low.shape[1]
    side = low.shape[0]
    blocks = rows // BLK
    return pl.pallas_call(
        block_kernel,
        out_shape=struct(rows, width),
        grid_spec=pltpu.PrefetchScalarGridSpec(
            num_scalar_prefetch=3,
            grid=(blocks,),
            in_specs=[
                pl.BlockSpec((BLK, width), lambda i, *_: (i, 0)),
                pl.BlockSpec(memory_space=pl.ANY),
                whole(low),
                whole(high),
                whole(gain),
                pl.BlockSpec((width, width), lambda i, *_: (0, 1)),
                pl.BlockSpec((width, width), lambda i, *_: (0, 2)),
            ],
            out_specs=pl.BlockSpec((BLK, width), lambda i, *_: (i, 0)),
            scratch_shapes=[
                pltpu.VMEM((2, rows + 2 * side, width), BF16),
                pltpu.SemaphoreType.DMA((2,)),
            ],
        ),
        compiler_params=params(),
        cost_estimate=cost(16 * rows * 5 * BLK * width, 12 * rows * width, rows * 5 * BLK * 12),
    )(ids, counts, live, projected, projected, low, high, gain, w_qkv, w_qkv)


def anchor_kernel(*refs):
    gain_ref, weight_ref, out_ref = refs[-3:]
    for part, rows_ref in enumerate(refs[:-3]):

        @pl.when(pl.program_id(0) == part)
        def _(rows_ref=rows_ref):
            tile = CHUNK
            for at in range(0, rows_ref.shape[0], tile):
                normed = normed_rows(rows_ref[at : at + tile, :], gain_ref[...])
                out_ref[at : at + tile, :] = mm(normed, weight_ref[...]).astype(BF16)


def anchor_project(parts, gain, weight):
    count, width = parts[0].shape
    every = len(parts) * count
    return pl.pallas_call(
        anchor_kernel,
        out_shape=struct(every, 2 * width),
        grid=(len(parts),),
        in_specs=[whole(part) for part in parts] + [whole(gain), whole(weight)],
        out_specs=pl.BlockSpec((count, 2 * width), lambda i: (i, 0)),
        compiler_params=params(),
        cost_estimate=cost(4 * every * width * width, 6 * every * width),
    )(*parts, gain, weight)


def sweep(query, keys_ref, values_ref):
    top, total = None, None
    for start in range(0, keys_ref.shape[0], CHUNK):
        scores = mm_t(query, keys_ref[start : start + CHUNK, :])
        values = values_ref[start : start + CHUNK, :]
        here = jnp.max(scores, axis=1, keepdims=True)
        if top is None:
            top = here
            total = weigh(jnp.exp2(scores - top), values)
        else:
            later = jnp.maximum(top, here)
            total = total * jnp.exp2(top - later) + weigh(jnp.exp2(scores - later), values)
            top = later
    sums = total[:, PAIR:]
    return join_heads(total[:, :PAIR] / sums), join_heads(top + jnp.log2(sums))


def cross_kernel(queries_ref, keys_ref, values_ref, mean_ref, size_ref):
    query = split_heads(queries_ref[...])
    mean_ref[...], size_ref[...] = sweep(query, keys_ref, values_ref)


def cross_part(projected, anchor_kv):
    rows = projected.shape[0]
    width = projected.shape[1] // 4
    count = anchor_kv.shape[0]
    pairs = width // PAIR
    tile = 512
    state = struct(rows, width, F32)
    spec = pl.BlockSpec((tile, PAIR), lambda h, i: (i, h))
    return pl.pallas_call(
        cross_kernel,
        out_shape=(state, state),
        grid=(pairs, rows // tile),
        in_specs=[
            pl.BlockSpec((tile, PAIR), lambda h, i: (i, 3 * pairs + h)),
            pl.BlockSpec((count, PAIR), lambda h, i: (0, h)),
            pl.BlockSpec((count, PAIR), lambda h, i: (0, pairs + h)),
        ],
        out_specs=[spec, spec],
        compiler_params=params(WIDE),
        cost_estimate=cost(16 * rows * count * width, 20 * rows * width, 12 * rows * count),
    )(projected, anchor_kv, anchor_kv)


def final_kernel(
    live_ref,
    queries_ref,
    keys_ref,
    values_ref,
    mean_ref,
    size_ref,
    block_ref,
    wout_ref,
    wcross_ref,
    out_ref,
    held_ref,
):
    pair = pl.program_id(1)
    rows = queries_ref.shape[0]
    query = split_heads(queries_ref[...])
    mean, size = sweep(query, keys_ref, values_ref)
    top = jnp.maximum(size, size_ref[...])
    share, other = jnp.exp2(size - top), jnp.exp2(size_ref[...] - top)
    held_ref[pair] = ((mean * share + mean_ref[...] * other) / (share + other)).astype(BF16)

    @pl.when(pair == pl.num_programs(1) - 1)
    def _():
        cross = jnp.concatenate([held_ref[n] for n in range(held_ref.shape[0])], axis=1)
        mixed = mm(block_ref[...], wout_ref[...]) + mm(cross, wcross_ref[...])
        place = lax.broadcasted_iota(jnp.int32, (rows, 1), 0) + pl.program_id(0) * rows
        out_ref[...] = jnp.where(place // BLK < live_ref[0], mixed, 0.0).astype(BF16)


def finish(projected, anchor_kv, state, block_attn, w_out, w_cross_out, live):
    rows = projected.shape[0]
    width = projected.shape[1] // 4
    count = anchor_kv.shape[0]
    pairs = width // PAIR
    tile = 512
    spec = pl.BlockSpec((tile, PAIR), lambda i, h, *_: (i, h))
    full = pl.BlockSpec((tile, width), lambda i, h, *_: (i, 0))
    return pl.pallas_call(
        final_kernel,
        out_shape=struct(rows, width),
        grid_spec=pltpu.PrefetchScalarGridSpec(
            num_scalar_prefetch=1,
            grid=(rows // tile, pairs),
            in_specs=[
                pl.BlockSpec((tile, PAIR), lambda i, h, *_: (i, 3 * pairs + h)),
                pl.BlockSpec((count, PAIR), lambda i, h, *_: (0, h)),
                pl.BlockSpec((count, PAIR), lambda i, h, *_: (0, pairs + h)),
                spec,
                spec,
                full,
                whole(w_out),
                whole(w_cross_out),
            ],
            out_specs=full,
            scratch_shapes=[pltpu.VMEM((pairs, tile, PAIR), BF16)],
        ),
        compiler_params=params(WIDE),
        cost_estimate=cost(16 * rows * count * width, 28 * rows * width, 12 * rows * count),
    )(live, projected, anchor_kv, anchor_kv, *state, block_attn, w_out, w_cross_out)


def after(*arrays):
    return lax.optimization_barrier(arrays)


def permute(array, target):
    size = lax.axis_size("dom")
    pairs = [(i, target(i)) for i in range(size) if 0 <= target(i) < size]
    return lax.ppermute(array, "dom", pairs)


def local(
    points,
    norm_gain,
    w_qkv,
    w_out,
    w_cross_q,
    w_cross_kv,
    w_cross_out,
    live_blocks,
    send_blocks,
    neighbours,
    neighbour_count,
    anchor_index,
):
    rows, width = points.shape
    gain = norm_gain.reshape(1, width)
    size = lax.axis_size("dom")
    column, ring = 2, 4
    anchors, to_prev, to_next = pick(points, send_blocks, anchor_index)

    def around(array):
        return [permute(array, lambda i, n=n: (i + n * ring) % size) for n in (1, -1, 2)]

    beside = permute(anchors, lambda i: i ^ column)
    low = permute(to_next, lambda i: i + 1)
    high = permute(to_prev, lambda i: i - 1)
    rows_here = around(anchors)
    points, anchors = after(points, anchors)
    projected = project(points, gain, w_qkv, w_cross_q)
    beside, projected = after(beside, projected)
    rows_beside = around(beside)
    block_attn = block_attention(
        projected, low, high, gain, w_qkv, neighbours, neighbour_count, live_blocks
    )
    *parts, block_attn = after(anchors, beside, *rows_here, *rows_beside, block_attn)
    kv_own = anchor_project(parts, gain, w_cross_kv)
    kv_other = permute(kv_own, lambda i: i ^ 1)
    state = cross_part(projected, kv_own)
    return finish(projected, kv_other, state, block_attn, w_out, w_cross_out, live_blocks)


def solution(mesh):
    sharded = P(("car", "dom"))
    in_specs = (
        P(("car", "dom"), None),
        P(),
        P(),
        P(),
        P(),
        P(),
        P(),
        sharded,
        sharded,
        P(("car", "dom"), None),
        sharded,
        sharded,
    )
    out_specs = P(("car", "dom"), None)
    return jax.shard_map(local, mesh=mesh, in_specs=in_specs, out_specs=out_specs, check_vma=False)
```

profile of v0, /device:TPU:1, one launch (start us, length us, event | category | flops | bytes accessed | tf_op | source)
XLA Modules:
  0.0 138.1 jit_solution(8443146307230162341)
XLA Ops:
  0.0 3.7 %shard_map.118 = (bf16[256,768]{1,0:T(8,128)(2,1)}, bf16[256,768]{1,0:T(8,128)(2,1)}, bf16[256,768]{1,0:T(8,128)(2,1)}) custom-call(s32[4]{0:T(128)} %send_ref.1, s32[1,256]{1,0:T(1,128)} %bitcast.1, bf16[1024,768]{1,0:T(8,128)(2,1)} %points_ref), custom_call_target="tpu_custom_call" | custom-call | flops 402653184 | bytes 3145728 | tf_op jit(solution)/shard_map/pallas_call | solution.py:77
  3.7 2.5 %collective-permute-start = (bf16[256,768]{1,0:T(8,128)(2,1)}, bf16[256,768]{1,0:T(8,128)(2,1)S(1)}, u32[]{:S(2)}, u32[]{:S(2)}) collective-permute-start(bf16[256,768]{1,0:T(8,128)(2,1)} %get-tuple-element.30.refs_0_), channel_id=1, source_target_pairs={{0,2},{1,3},{2,0},{3,1},{4,6},{5,7},{6,4},{7,5},{8,10},{9,11},{10,... | collective-permute-start | bytes 1179656 | tf_op jit(solution)/shard_map/ppermute | solution.py:399
  6.2 1.3 collective-permute-start.1
  7.5 1.4 %collective-permute-start.2 = (bf16[256,768]{1,0:T(8,128)(2,1)}, bf16[256,768]{1,0:T(8,128)(2,1)S(1)}, u32[]{:S(2)}, u32[]{:S(2)}) collective-permute-start(bf16[256,768]{1,0:T(8,128)(2,1)} %get-tuple-element.30.refs_0_), channel_id=1, source_target_pairs={{0,12},{1,13},{2,14},{3,15},{4,0},{5,1},{6,2},{7,3},{8,4},{9,5},{1... | collective-permute-start | bytes 1179656 | tf_op jit(solution)/shard_map/ppermute | solution.py:399
  9.0 3.0 %collective-permute-start.7 = (bf16[256,768]{1,0:T(8,128)(2,1)}, bf16[256,768]{1,0:T(8,128)(2,1)S(1)}, u32[]{:S(2)}, u32[]{:S(2)}) collective-permute-start(bf16[256,768]{1,0:T(8,128)(2,1)} %get-tuple-element.28), channel_id=1, source_target_pairs={{0,1},{1,2},{2,3},{3,4},{4,5},{5,6},{6,7},{7,8},{8,9},{9,10},{10,1... | collective-permute-start | bytes 1179656 | tf_op jit(solution)/shard_map/ppermute | solution.py:399
  12.0 1.9 %collective-permute-start.8 = (bf16[256,768]{1,0:T(8,128)(2,1)}, bf16[256,768]{1,0:T(8,128)(2,1)S(1)}, u32[]{:S(2)}, u32[]{:S(2)}) collective-permute-start(bf16[256,768]{1,0:T(8,128)(2,1)} %get-tuple-element.29), channel_id=1, source_target_pairs={{1,0},{2,1},{3,2},{4,3},{5,4},{6,5},{7,6},{8,7},{9,8},{10,9},{11,1... | collective-permute-start | bytes 1179656 | tf_op jit(solution)/shard_map/ppermute | solution.py:399
  14.6 0.7 reshape.7.gain_ref.refs_8_
  15.3 1.4 %copy-done = bf16[1024,768]{1,0:T(8,128)(2,1)S(1)} copy-done((bf16[1024,768]{1,0:T(8,128)(2,1)S(1)}, bf16[1024,768]{1,0:T(8,128)(2,1)}, u32[]{:S(2)}) %copy-start) | copy-done | bytes 1572888
  16.7 2.0 %copy-done.1 = bf16[768,2304]{1,0:T(8,128)(2,1)S(1)} copy-done((bf16[768,2304]{1,0:T(8,128)(2,1)S(1)}, bf16[768,2304]{1,0:T(8,128)(2,1)}, u32[]{:S(2)}) %copy-start.1) | copy-done | bytes 3538968
  18.7 1.3 copy-done.4
  20.0 6.5 %shard_map.119.queries_ref.projected_ref = bf16[1024,3072]{1,0:T(8,128)(2,1)S(1)} custom-call(bf16[1024,768]{1,0:T(8,128)(2,1)S(1)} %copy-done, f32[1,768]{1,0:T(1,128)S(1)} %reshape.7.gain_ref.refs_8_, bf16[768,2304]{1,0:T(8,128)(2,1)S(1)} %copy-done.1, bf16[768,768]{1,0:T(8,128)(2,1)S(1)} %copy-done.4), custom_call_target="tpu_custom_call" | custom-call | flops 4831838208 | bytes 15728640 | tf_op jit(solution)/shard_map/pallas_call | solution.py:114
  26.5 0.0 copy-start.3
  26.5 2.1 %collective-permute-start.3 = (bf16[256,768]{1,0:T(8,128)(2,1)S(1)}, bf16[256,768]{1,0:T(8,128)(2,1)S(1)}, u32[]{:S(2)}, u32[]{:S(2)}) collective-permute-start(bf16[256,768]{1,0:T(8,128)(2,1)S(1)} %copy-done.5), channel_id=1, source_target_pairs={{0,8},{1,9},{2,10},{3,11},{4,12},{5,13},{6,14},{7,15},{8,0},{9,1},... | collective-permute-start | bytes 1179656 | tf_op jit(solution)/shard_map/ppermute | solution.py:399
  28.6 0.4 collective-permute-start.4
  29.0 2.3 %collective-permute-start.5 = (bf16[256,768]{1,0:T(8,128)(2,1)S(1)}, bf16[256,768]{1,0:T(8,128)(2,1)S(1)}, u32[]{:S(2)}, u32[]{:S(2)}) collective-permute-start(bf16[256,768]{1,0:T(8,128)(2,1)S(1)} %collective-permute-done.refs_1_), channel_id=1, source_target_pairs={{0,12},{1,13},{2,14},{3,15},{4,0},{5,1},{6,2},{7,3},{8,4},{9,5},{1... | collective-permute-start | bytes 1179656 | tf_op jit(solution)/shard_map/ppermute | solution.py:399
  31.3 0.0 collective-permute-start.6
  31.3 14.0 %shard_map.120.block_ref = bf16[1024,768]{1,0:T(8,128)(2,1)S(1)} custom-call(s32[8,8]{1,0:T(8,128)S(1)} %copy-done.6, s32[8]{0:T(128)S(1)} %copy-done.7, s32[1]{0:T(128)S(6)} %copy.13.live_ref, bf16[1024,3072]{1,0:T(8,128)(2,1)S(1)} %shard_map.119.queries_ref.projected_ref, bf16[1024,3072]{1,0:T(8,128)(2,1)S(1)} %shard_map.119.queries_ref.projected_ref, ...), custom_call_target="tpu_custom_call" | custom-call | flops 8053063680 | bytes 9437184 | tf_op jit(solution)/shard_map/pallas_call | solution.py:234
  45.3 0.0 collective-permute-done.2.refs_3_
  45.3 4.0 %collective-permute-done.4.refs_5_ = bf16[256,768]{1,0:T(8,128)(2,1)S(1)} collective-permute-done((bf16[256,768]{1,0:T(8,128)(2,1)S(1)}, bf16[256,768]{1,0:T(8,128)(2,1)S(1)}, u32[]{:S(2)}, u32[]{:S(2)}) %collective-permute-start.4) | collective-permute-done | bytes 393248 | tf_op jit(solution)/shard_map/ppermute | solution.py:399
  49.4 4.8 %collective-permute-done.6.refs_7_ = bf16[256,768]{1,0:T(8,128)(2,1)S(1)} collective-permute-done((bf16[256,768]{1,0:T(8,128)(2,1)S(1)}, bf16[256,768]{1,0:T(8,128)(2,1)S(1)}, u32[]{:S(2)}, u32[]{:S(2)}) %collective-permute-start.6) | collective-permute-done | bytes 393248 | tf_op jit(solution)/shard_map/ppermute | solution.py:399
  54.2 8.1 %shard_map.121.keys_ref.values_ref = bf16[2048,1536]{1,0:T(8,128)(2,1)} custom-call(bf16[256,768]{1,0:T(8,128)(2,1)S(1)} %copy-done.5, bf16[256,768]{1,0:T(8,128)(2,1)S(1)} %collective-permute-done.refs_1_, bf16[256,768]{1,0:T(8,128)(2,1)S(1)} %collective-permute-done.1.refs_2_, bf16[256,768]{1,0:T(8,128)(2,1)S(1)} %collective-permute-done.2.refs_3_, ...), custom_call_target="tpu_custom_call" | custom-call | flops 4831838208 | bytes 9437184 | tf_op jit(solution)/shard_map/pallas_call | solution.py:275
  62.3 2.3 %collective-permute-start.9 = (bf16[2048,1536]{1,0:T(8,128)(2,1)}, bf16[2048,1536]{1,0:T(8,128)(2,1)}, u32[]{:S(2)}, u32[]{:S(2)}) collective-permute-start(bf16[2048,1536]{1,0:T(8,128)(2,1)} %shard_map.121.keys_ref.values_ref), channel_id=1, source_target_pairs={{0,1},{1,0},{2,3},{3,2},{4,5},{5,4},{6,7},{7,6},{8,9},{9,8},{10,11... | collective-permute-start | bytes 18874376 | tf_op jit(solution)/shard_map/ppermute | solution.py:399
  64.6 33.8 %shard_map.122 = (f32[1024,768]{1,0:T(8,128)}, f32[1024,768]{1,0:T(8,128)}) custom-call(bf16[1024,3072]{1,0:T(8,128)(2,1)} %copy-done.8, bf16[2048,1536]{1,0:T(8,128)(2,1)} %shard_map.121.keys_ref.values_ref, bf16[2048,1536]{1,0:T(8,128)(2,1)} %shard_map.121.keys_ref.values_ref), custom_call_target="tpu_custom_call" | custom-call | flops 25769803776 | bytes 15728640 | tf_op jit(solution)/shard_map/pallas_call | solution.py:316
  98.5 39.7 %shard_map.123 = bf16[1024,768]{1,0:T(8,128)(2,1)} custom-call(s32[1]{0:T(128)S(6)} %copy.13.live_ref, bf16[1024,3072]{1,0:T(8,128)(2,1)} %copy-done.8, bf16[2048,1536]{1,0:T(8,128)(2,1)} %collective-permute-done.9.keys_ref.values_ref, bf16[2048,1536]{1,0:T(8,128)(2,1)} %collective-permute-done.9.keys_ref.values_ref, ...), custom_call_target="tpu_custom_call" | custom-call | flops 25769803776 | bytes 22020096 | tf_op jit(solution)/shard_map/pallas_call | solution.py:368
  (23 shorter events, 0.0 us)
Async XLA Ops:
  3.7 22.8 %collective-permute-start = (bf16[256,768]{1,0:T(8,128)(2,1)}, bf16[256,768]{1,0:T(8,128)(2,1)S(1)}, u32[]{:S(2)}, u32[]{:S(2)}) collective-permute-start(bf16[256,768]{1,0:T(8,128)(2,1)} %get-tuple-element.30.refs_0_), channel_id=1, source_target_pairs={{0,2},{1,3},{2,0},{3,1},{4,6},{5,7},{6,4},{7,5},{8,10},{9,11},{10,... | collective-permute-start | bytes 1179656 | tf_op jit(solution)/shard_map/ppermute | solution.py:399
  6.2 22.4 %collective-permute-start.1 = (bf16[256,768]{1,0:T(8,128)(2,1)}, bf16[256,768]{1,0:T(8,128)(2,1)S(1)}, u32[]{:S(2)}, u32[]{:S(2)}) collective-permute-start(bf16[256,768]{1,0:T(8,128)(2,1)} %get-tuple-element.30.refs_0_), channel_id=1, source_target_pairs={{0,4},{1,5},{2,6},{3,7},{4,8},{5,9},{6,10},{7,11},{8,12},{9,13},{1... | collective-permute-start | bytes 1179656 | tf_op jit(solution)/shard_map/ppermute | solution.py:399
  7.5 37.8 %collective-permute-start.2 = (bf16[256,768]{1,0:T(8,128)(2,1)}, bf16[256,768]{1,0:T(8,128)(2,1)S(1)}, u32[]{:S(2)}, u32[]{:S(2)}) collective-permute-start(bf16[256,768]{1,0:T(8,128)(2,1)} %get-tuple-element.30.refs_0_), channel_id=1, source_target_pairs={{0,12},{1,13},{2,14},{3,15},{4,0},{5,1},{6,2},{7,3},{8,4},{9,5},{1... | collective-permute-start | bytes 1179656 | tf_op jit(solution)/shard_map/ppermute | solution.py:399
  9.0 20.1 %collective-permute-start.7 = (bf16[256,768]{1,0:T(8,128)(2,1)}, bf16[256,768]{1,0:T(8,128)(2,1)S(1)}, u32[]{:S(2)}, u32[]{:S(2)}) collective-permute-start(bf16[256,768]{1,0:T(8,128)(2,1)} %get-tuple-element.28), channel_id=1, source_target_pairs={{0,1},{1,2},{2,3},{3,4},{4,5},{5,6},{6,7},{7,8},{8,9},{9,10},{10,1... | collective-permute-start | bytes 1179656 | tf_op jit(solution)/shard_map/ppermute | solution.py:399
  12.0 19.3 %collective-permute-start.8 = (bf16[256,768]{1,0:T(8,128)(2,1)}, bf16[256,768]{1,0:T(8,128)(2,1)S(1)}, u32[]{:S(2)}, u32[]{:S(2)}) collective-permute-start(bf16[256,768]{1,0:T(8,128)(2,1)} %get-tuple-element.29), channel_id=1, source_target_pairs={{1,0},{2,1},{3,2},{4,3},{5,4},{6,5},{7,6},{8,7},{9,8},{10,9},{11,1... | collective-permute-start | bytes 1179656 | tf_op jit(solution)/shard_map/ppermute | solution.py:399
  15.3 1.4 %copy-start = (bf16[1024,768]{1,0:T(8,128)(2,1)S(1)}, bf16[1024,768]{1,0:T(8,128)(2,1)}, u32[]{:S(2)}) copy-start(bf16[1024,768]{1,0:T(8,128)(2,1)} %points_ref) | copy-start | bytes 4718596
  16.7 2.0 %copy-start.1 = (bf16[768,2304]{1,0:T(8,128)(2,1)S(1)}, bf16[768,2304]{1,0:T(8,128)(2,1)}, u32[]{:S(2)}) copy-start(bf16[768,2304]{1,0:T(8,128)(2,1)} %wv_ref.1) | copy-start | bytes 10616836
  18.7 1.3 copy-start.4
  20.0 6.5 %copy-start.5 = (bf16[256,768]{1,0:T(8,128)(2,1)S(1)}, bf16[256,768]{1,0:T(8,128)(2,1)}, u32[]{:S(2)}) copy-start(bf16[256,768]{1,0:T(8,128)(2,1)} %get-tuple-element.30.refs_0_) | copy-start | bytes 1179652
  20.0 11.3 %copy-start.2 = (bf16[768,2304]{1,0:T(8,128)(2,1)S(1)}, bf16[768,2304]{1,0:T(8,128)(2,1)}, u32[]{:S(2)}) copy-start(bf16[768,2304]{1,0:T(8,128)(2,1)} %wv_ref.1) | copy-start | bytes 10616836
  20.0 11.4 %copy-start.6 = (s32[8,8]{1,0:T(8,128)S(1)}, s32[8,8]{1,0:T(8,128)}, u32[]{:S(2)}) copy-start(s32[8,8]{1,0:T(8,128)} %ids_ref.1) | copy-start | bytes 772
  20.0 11.4 %copy-start.7 = (s32[8]{0:T(128)S(1)}, s32[8]{0:T(128)}, u32[]{:S(2)}) copy-start(s32[8]{0:T(128)} %count_ref.1) | copy-start | bytes 100
  26.5 18.8 %copy-start.8 = (bf16[1024,3072]{1,0:T(8,128)(2,1)}, bf16[1024,3072]{1,0:T(8,128)(2,1)S(1)}, u32[]{:S(2)}) copy-start(bf16[1024,3072]{1,0:T(8,128)(2,1)S(1)} %shard_map.119.queries_ref.projected_ref) | copy-start | bytes 18874372
  26.5 27.7 %copy-start.3 = (bf16[768,1536]{1,0:T(8,128)(2,1)S(1)}, bf16[768,1536]{1,0:T(8,128)(2,1)}, u32[]{:S(2)}) copy-start(bf16[768,1536]{1,0:T(8,128)(2,1)} %refs_9_.1) | copy-start | bytes 7077892
  26.5 18.8 %collective-permute-start.3 = (bf16[256,768]{1,0:T(8,128)(2,1)S(1)}, bf16[256,768]{1,0:T(8,128)(2,1)S(1)}, u32[]{:S(2)}, u32[]{:S(2)}) collective-permute-start(bf16[256,768]{1,0:T(8,128)(2,1)S(1)} %copy-done.5), channel_id=1, source_target_pairs={{0,8},{1,9},{2,10},{3,11},{4,12},{5,13},{6,14},{7,15},{8,0},{9,1},... | collective-permute-start | bytes 1179656 | tf_op jit(solution)/shard_map/ppermute | solution.py:399
  28.6 20.7 %collective-permute-start.4 = (bf16[256,768]{1,0:T(8,128)(2,1)S(1)}, bf16[256,768]{1,0:T(8,128)(2,1)S(1)}, u32[]{:S(2)}, u32[]{:S(2)}) collective-permute-start(bf16[256,768]{1,0:T(8,128)(2,1)S(1)} %collective-permute-done.refs_1_), channel_id=1, source_target_pairs={{0,4},{1,5},{2,6},{3,7},{4,8},{5,9},{6,10},{7,11},{8,12},{9,13},{1... | collective-permute-start | bytes 1179656 | tf_op jit(solution)/shard_map/ppermute | solution.py:399
  29.0 20.3 %collective-permute-start.5 = (bf16[256,768]{1,0:T(8,128)(2,1)S(1)}, bf16[256,768]{1,0:T(8,128)(2,1)S(1)}, u32[]{:S(2)}, u32[]{:S(2)}) collective-permute-start(bf16[256,768]{1,0:T(8,128)(2,1)S(1)} %collective-permute-done.refs_1_), channel_id=1, source_target_pairs={{0,12},{1,13},{2,14},{3,15},{4,0},{5,1},{6,2},{7,3},{8,4},{9,5},{1... | collective-permute-start | bytes 1179656 | tf_op jit(solution)/shard_map/ppermute | solution.py:399
  31.3 22.9 %collective-permute-start.6 = (bf16[256,768]{1,0:T(8,128)(2,1)S(1)}, bf16[256,768]{1,0:T(8,128)(2,1)S(1)}, u32[]{:S(2)}, u32[]{:S(2)}) collective-permute-start(bf16[256,768]{1,0:T(8,128)(2,1)S(1)} %collective-permute-done.refs_1_), channel_id=1, source_target_pairs={{0,8},{1,9},{2,10},{3,11},{4,12},{5,13},{6,14},{7,15},{8,0},{9,1},... | collective-permute-start | bytes 1179656 | tf_op jit(solution)/shard_map/ppermute | solution.py:399
  45.3 17.0 %copy-start.9 = (bf16[1024,768]{1,0:T(8,128)(2,1)}, bf16[1024,768]{1,0:T(8,128)(2,1)S(1)}, u32[]{:S(2)}) copy-start(bf16[1024,768]{1,0:T(8,128)(2,1)S(1)} %shard_map.120.block_ref) | copy-start | bytes 4718596
  62.3 36.2 %collective-permute-start.9 = (bf16[2048,1536]{1,0:T(8,128)(2,1)}, bf16[2048,1536]{1,0:T(8,128)(2,1)}, u32[]{:S(2)}, u32[]{:S(2)}) collective-permute-start(bf16[2048,1536]{1,0:T(8,128)(2,1)} %shard_map.121.keys_ref.values_ref), channel_id=1, source_target_pairs={{0,1},{1,0},{2,3},{3,2},{4,5},{5,4},{6,7},{7,6},{8,9},{9,8},{10,11... | collective-permute-start | bytes 18874376 | tf_op jit(solution)/shard_map/ppermute | solution.py:399
where the time goes:
time: 138 us
  Pallas kernels  106 us (77%)
  starting transfers between devices  17.3 us (13%)
  waiting for transfers between devices  8.88 us (6%)
  local copies, waits for them, and re-layouts  5.4 us (4%)
    pallas_call x1, Pallas kernels, finish(): pl.pallas_call(final_kernel, out_shape=struct(rows, width), grid_spec=plt...  39.7 us
    pallas_call x1, Pallas kernels, cross_part(): pl.pallas_call(cross_kernel, out_shape=(state, state), grid=(pairs, rows...  33.8 us
    ppermute x10, starting transfers between devices, permute(): return lax.ppermute(array, 'dom', pairs)  17.3 us
    pallas_call x1, Pallas kernels, block_attention(): pl.pallas_call(block_kernel, out_shape=struct(rows, width), grid_spec=plt...  14 us
    ppermute x10, waiting for transfers between devices, permute(): return lax.ppermute(array, 'dom', pairs)  8.88 us
    pallas_call x1, Pallas kernels, anchor_project(): pl.pallas_call(anchor_kernel, out_shape=struct(every, 2 * width), grid=(l...  8.09 us
    pallas_call x1, Pallas kernels, project(): pl.pallas_call(project_kernel, out_shape=struct(rows, 4 * width), grid=(4...  6.5 us
    unnamed x20, local copies, waits for them, and re-layouts  4.71 us
  transfers between devices with their start and end apart: 10, of which 2 were waited for; matrix products, arithmetic and copies ran while one was open for 1% of the time, Pallas kernels for 39%

commit v1 on v0

--- a/solution.py
+++ b/solution.py
@@ -257,27 +257,41 @@
     )(ids, counts, live, projected, projected, low, high, gain, w_qkv, w_qkv)
 
 
-def anchor_kernel(*refs):
-    gain_ref, weight_ref, out_ref = refs[-3:]
-    for part, rows_ref in enumerate(refs[:-3]):
-
-        @pl.when(pl.program_id(0) == part)
-        def _(rows_ref=rows_ref):
-            tile = CHUNK
-            for at in range(0, rows_ref.shape[0], tile):
-                normed = normed_rows(rows_ref[at : at + tile, :], gain_ref[...])
-                out_ref[at : at + tile, :] = mm(normed, weight_ref[...]).astype(BF16)
+def anchor_kernel(count, *refs):
+    parts = refs[:count]
+    gain_ref, weight_ref, out_ref, held_ref, sems = refs[count:]
+    rows = parts[0].shape[0]
+    normed = normed_rows(parts[0][...], gain_ref[...])
+    stores = []
+    for part in range(count):
+        slot = part % 2
+        if part >= 2:
+            stores[part - 2].wait()
+        held_ref[slot] = mm(normed, weight_ref[...]).astype(BF16)
+        if part + 1 < count:
+            normed = normed_rows(parts[part + 1][...], gain_ref[...])
+        store = pltpu.make_async_copy(
+            held_ref.at[slot], out_ref.at[part * rows : (part + 1) * rows], sems.at[slot]
+        )
+        store.start()
+        stores.append(store)
+    for store in stores[-2:]:
+        store.wait()
 
 
 def anchor_project(parts, gain, weight):
-    count, width = parts[0].shape
-    every = len(parts) * count
-    return pl.pallas_call(
-        anchor_kernel,
+    rows, width = parts[0].shape
+    every = len(parts) * rows
+    vmem = pl.BlockSpec(memory_space=pltpu.VMEM)
+    return pl.pallas_call(
+        functools.partial(anchor_kernel, len(parts)),
         out_shape=struct(every, 2 * width),
-        grid=(len(parts),),
-        in_specs=[whole(part) for part in parts] + [whole(gain), whole(weight)],
-        out_specs=pl.BlockSpec((count, 2 * width), lambda i: (i, 0)),
+        in_specs=[vmem] * (len(parts) + 2),
+        out_specs=pl.BlockSpec(memory_space=pltpu.HBM),
+        scratch_shapes=[
+            pltpu.VMEM((2, rows, 2 * width), BF16),
+            pltpu.SemaphoreType.DMA((2,)),
+        ],
         compiler_params=params(),
         cost_estimate=cost(4 * every * width * width, 6 * every * width),
     )(*parts, gain, weight)
@@ -428,8 +442,11 @@
     rows_here = around(anchors)
     points, anchors = after(points, anchors)
     projected = project(points, gain, w_qkv, w_cross_q)
-    beside, projected = after(beside, projected)
-    rows_beside = around(beside)
+    beside, rows_here[0], rows_here[1], projected = after(
+        beside, rows_here[0], rows_here[1], projected
+    )
+    rows_beside = [permute(rows_here[n], lambda i: i ^ column) for n in range(2)]
+    rows_beside.append(permute(beside, lambda i: (i + 2 * ring) % size))
     block_attn = block_attention(
         projected, low, high, gain, w_qkv, neighbours, neighbour_count, live_blocks
     )

time: 138 us -> 133 us (0.964); the launches traced: 138 us -> 131 us
  waiting for transfers between devices: 8.88 us -> 2.36 us
    ppermute x10, waiting for transfers between devices: 8.88 us -> 2.36 us  [permute(): return lax.ppermute(array, 'dom', pairs)]
  transfers between devices with their start and end apart: 10 -> 10, of which waited for: 2 -> 1; matrix products, arithmetic and copies ran while one was open for 1% -> 1% of each run, Pallas kernels for 39% -> 41%
where the time goes in v1:
time: 133 us; the launch traced here: 131 us
  Pallas kernels  105 us (79%)
  starting transfers between devices  17.3 us (13%)
  local copies, waits for them, and re-layouts  5.4 us (4%)
  waiting for transfers between devices  2.36 us (2%)
    pallas_call x1, Pallas kernels, finish(): pl.pallas_call(final_kernel, out_shape=struct(rows, width), grid_spec=plt...  39.7 us
    pallas_call x1, Pallas kernels, cross_part(): pl.pallas_call(cross_kernel, out_shape=(state, state), grid=(pairs, rows...  33.8 us
    ppermute x10, starting transfers between devices, permute(): return lax.ppermute(array, 'dom', pairs)  17.3 us
    pallas_call x1, Pallas kernels, block_attention(): pl.pallas_call(block_kernel, out_shape=struct(rows, width), grid_spec=plt...  13.5 us
    pallas_call x1, Pallas kernels, anchor_project(): pl.pallas_call(functools.partial(anchor_kernel, len(parts)), out_shape=st...  7.62 us
    pallas_call x1, Pallas kernels, project(): pl.pallas_call(project_kernel, out_shape=struct(rows, 4 * width), grid=(4...  6.5 us
    unnamed x20, local copies, waits for them, and re-layouts  4.71 us
    pallas_call x1, Pallas kernels, pick(): pl.pallas_call(pick_kernel, out_shape=(own, side, side), in_specs=[pl.Blo...  3.67 us
  transfers between devices with their start and end apart: 10, of which 1 were waited for; matrix products, arithmetic and copies ran while one was open for 1% of the time, Pallas kernels for 41%

profile of v1, /device:TPU:1, one launch (start us, length us, event | category | flops | bytes accessed | tf_op | source)
XLA Modules:
  0.0 130.6 jit_solution(396747998537723670)
XLA Ops:
  0.0 3.7 %shard_map.118 = (bf16[256,768]{1,0:T(8,128)(2,1)}, bf16[256,768]{1,0:T(8,128)(2,1)}, bf16[256,768]{1,0:T(8,128)(2,1)}) custom-call(s32[4]{0:T(128)} %send_ref.1, s32[1,256]{1,0:T(1,128)} %bitcast.1, bf16[1024,768]{1,0:T(8,128)(2,1)} %points_ref), custom_call_target="tpu_custom_call" | custom-call | flops 402653184 | bytes 3145728 | tf_op jit(solution)/shard_map/pallas_call | solution.py:77
  3.7 2.5 %collective-permute-start = (bf16[256,768]{1,0:T(8,128)(2,1)}, bf16[256,768]{1,0:T(8,128)(2,1)S(1)}, u32[]{:S(2)}, u32[]{:S(2)}) collective-permute-start(bf16[256,768]{1,0:T(8,128)(2,1)} %get-tuple-element.34.refs_0_), channel_id=1, source_target_pairs={{0,2},{1,3},{2,0},{3,1},{4,6},{5,7},{6,4},{7,5},{8,10},{9,11},{10,... | collective-permute-start | bytes 1179656 | tf_op jit(solution)/shard_map/ppermute | solution.py:413
  6.2 1.3 collective-permute-start.1
  7.5 1.4 %collective-permute-start.2 = (bf16[256,768]{1,0:T(8,128)(2,1)}, bf16[256,768]{1,0:T(8,128)(2,1)S(1)}, u32[]{:S(2)}, u32[]{:S(2)}) collective-permute-start(bf16[256,768]{1,0:T(8,128)(2,1)} %get-tuple-element.34.refs_0_), channel_id=1, source_target_pairs={{0,12},{1,13},{2,14},{3,15},{4,0},{5,1},{6,2},{7,3},{8,4},{9,5},{1... | collective-permute-start | bytes 1179656 | tf_op jit(solution)/shard_map/ppermute | solution.py:413
  9.0 3.0 %collective-permute-start.7 = (bf16[256,768]{1,0:T(8,128)(2,1)}, bf16[256,768]{1,0:T(8,128)(2,1)S(1)}, u32[]{:S(2)}, u32[]{:S(2)}) collective-permute-start(bf16[256,768]{1,0:T(8,128)(2,1)} %get-tuple-element.32), channel_id=1, source_target_pairs={{0,1},{1,2},{2,3},{3,4},{4,5},{5,6},{6,7},{7,8},{8,9},{9,10},{10,1... | collective-permute-start | bytes 1179656 | tf_op jit(solution)/shard_map/ppermute | solution.py:413
  12.0 1.9 %collective-permute-start.8 = (bf16[256,768]{1,0:T(8,128)(2,1)}, bf16[256,768]{1,0:T(8,128)(2,1)S(1)}, u32[]{:S(2)}, u32[]{:S(2)}) collective-permute-start(bf16[256,768]{1,0:T(8,128)(2,1)} %get-tuple-element.33), channel_id=1, source_target_pairs={{1,0},{2,1},{3,2},{4,3},{5,4},{6,5},{7,6},{8,7},{9,8},{10,9},{11,1... | collective-permute-start | bytes 1179656 | tf_op jit(solution)/shard_map/ppermute | solution.py:413
  14.6 0.7 reshape.7.gain_ref.refs_8_
  15.3 1.4 %copy-done = bf16[1024,768]{1,0:T(8,128)(2,1)S(1)} copy-done((bf16[1024,768]{1,0:T(8,128)(2,1)S(1)}, bf16[1024,768]{1,0:T(8,128)(2,1)}, u32[]{:S(2)}) %copy-start) | copy-done | bytes 1572888
  16.7 2.0 %copy-done.1 = bf16[768,2304]{1,0:T(8,128)(2,1)S(1)} copy-done((bf16[768,2304]{1,0:T(8,128)(2,1)S(1)}, bf16[768,2304]{1,0:T(8,128)(2,1)}, u32[]{:S(2)}) %copy-start.1) | copy-done | bytes 3538968
  18.7 1.3 copy-done.4
  20.0 6.5 %shard_map.119.queries_ref.projected_ref = bf16[1024,3072]{1,0:T(8,128)(2,1)S(1)} custom-call(bf16[1024,768]{1,0:T(8,128)(2,1)S(1)} %copy-done, f32[1,768]{1,0:T(1,128)S(1)} %reshape.7.gain_ref.refs_8_, bf16[768,2304]{1,0:T(8,128)(2,1)S(1)} %copy-done.1, bf16[768,768]{1,0:T(8,128)(2,1)S(1)} %copy-done.4), custom_call_target="tpu_custom_call" | custom-call | flops 4831838208 | bytes 15728640 | tf_op jit(solution)/shard_map/pallas_call | solution.py:114
  26.5 0.0 copy-start.3
  26.5 0.0 collective-permute-done.refs_1_
  26.5 2.1 %collective-permute-start.3 = (bf16[256,768]{1,0:T(8,128)(2,1)S(1)}, bf16[256,768]{1,0:T(8,128)(2,1)S(1)}, u32[]{:S(2)}, u32[]{:S(2)}) collective-permute-start(bf16[256,768]{1,0:T(8,128)(2,1)S(1)} %copy-done.5), channel_id=1, source_target_pairs={{0,8},{1,9},{2,10},{3,11},{4,12},{5,13},{6,14},{7,15},{8,0},{9,1},... | collective-permute-start | bytes 1179656 | tf_op jit(solution)/shard_map/ppermute | solution.py:413
  28.6 0.0 collective-permute-done.1.refs_2_
  28.6 2.1 %collective-permute-start.4 = (bf16[256,768]{1,0:T(8,128)(2,1)S(1)}, bf16[256,768]{1,0:T(8,128)(2,1)S(1)}, u32[]{:S(2)}, u32[]{:S(2)}) collective-permute-start(bf16[256,768]{1,0:T(8,128)(2,1)S(1)} %collective-permute-done.1.refs_2_), channel_id=1, source_target_pairs={{0,2},{1,3},{2,0},{3,1},{4,6},{5,7},{6,4},{7,5},{8,10},{9,11},{10,... | collective-permute-start | bytes 1179656 | tf_op jit(solution)/shard_map/ppermute | solution.py:413
  30.7 0.1 collective-permute-start.5
  30.8 0.3 collective-permute-start.6
  31.2 13.5 %shard_map.120.block_ref = bf16[1024,768]{1,0:T(8,128)(2,1)S(1)} custom-call(s32[8,8]{1,0:T(8,128)S(1)} %copy-done.6, s32[8]{0:T(128)S(1)} %copy-done.7, s32[1]{0:T(128)S(6)} %copy.13.live_ref, bf16[1024,3072]{1,0:T(8,128)(2,1)S(1)} %shard_map.119.queries_ref.projected_ref, bf16[1024,3072]{1,0:T(8,128)(2,1)S(1)} %shard_map.119.queries_ref.projected_ref, ...), custom_call_target="tpu_custom_call" | custom-call | flops 8053063680 | bytes 9437184 | tf_op jit(solution)/shard_map/pallas_call | solution.py:234
  44.7 2.3 %collective-permute-done.5.refs_6_ = bf16[256,768]{1,0:T(8,128)(2,1)S(1)} collective-permute-done((bf16[256,768]{1,0:T(8,128)(2,1)S(1)}, bf16[256,768]{1,0:T(8,128)(2,1)S(1)}, u32[]{:S(2)}, u32[]{:S(2)}) %collective-permute-start.5) | collective-permute-done | bytes 393248 | tf_op jit(solution)/shard_map/ppermute | solution.py:413
  47.0 7.6 %shard_map.121.keys_ref.values_ref = bf16[2048,1536]{1,0:T(8,128)(2,1)} custom-call(bf16[256,768]{1,0:T(8,128)(2,1)S(1)} %copy-done.5, bf16[256,768]{1,0:T(8,128)(2,1)S(1)} %collective-permute-done.refs_1_, bf16[256,768]{1,0:T(8,128)(2,1)S(1)} %collective-permute-done.1.refs_2_, bf16[256,768]{1,0:T(8,128)(2,1)S(1)} %collective-permute-done.2.refs_3_, ...), custom_call_target="tpu_custom_call" | custom-call | flops 4831838208 | bytes 9437184 | tf_op jit(solution)/shard_map/pallas_call | solution.py:286
  54.6 2.5 %collective-permute-start.9 = (bf16[2048,1536]{1,0:T(8,128)(2,1)}, bf16[2048,1536]{1,0:T(8,128)(2,1)}, u32[]{:S(2)}, u32[]{:S(2)}) collective-permute-start(bf16[2048,1536]{1,0:T(8,128)(2,1)} %shard_map.121.keys_ref.values_ref), channel_id=1, source_target_pairs={{0,1},{1,0},{2,3},{3,2},{4,5},{5,4},{6,7},{7,6},{8,9},{9,8},{10,11... | collective-permute-start | bytes 18874376 | tf_op jit(solution)/shard_map/ppermute | solution.py:413
  57.1 33.8 %shard_map.122 = (f32[1024,768]{1,0:T(8,128)}, f32[1024,768]{1,0:T(8,128)}) custom-call(bf16[1024,3072]{1,0:T(8,128)(2,1)} %copy-done.8, bf16[2048,1536]{1,0:T(8,128)(2,1)} %shard_map.121.keys_ref.values_ref, bf16[2048,1536]{1,0:T(8,128)(2,1)} %shard_map.121.keys_ref.values_ref), custom_call_target="tpu_custom_call" | custom-call | flops 25769803776 | bytes 15728640 | tf_op jit(solution)/shard_map/pallas_call | solution.py:330
  91.0 39.7 %shard_map.123 = bf16[1024,768]{1,0:T(8,128)(2,1)} custom-call(s32[1]{0:T(128)S(6)} %copy.13.live_ref, bf16[1024,3072]{1,0:T(8,128)(2,1)} %copy-done.8, bf16[2048,1536]{1,0:T(8,128)(2,1)} %collective-permute-done.9.keys_ref.values_ref, bf16[2048,1536]{1,0:T(8,128)(2,1)} %collective-permute-done.9.keys_ref.values_ref, ...), custom_call_target="tpu_custom_call" | custom-call | flops 25769803776 | bytes 22020096 | tf_op jit(solution)/shard_map/pallas_call | solution.py:382
  (23 shorter events, 0.0 us)
Async XLA Ops:
  3.7 22.8 %collective-permute-start = (bf16[256,768]{1,0:T(8,128)(2,1)}, bf16[256,768]{1,0:T(8,128)(2,1)S(1)}, u32[]{:S(2)}, u32[]{:S(2)}) collective-permute-start(bf16[256,768]{1,0:T(8,128)(2,1)} %get-tuple-element.34.refs_0_), channel_id=1, source_target_pairs={{0,2},{1,3},{2,0},{3,1},{4,6},{5,7},{6,4},{7,5},{8,10},{9,11},{10,... | collective-permute-start | bytes 1179656 | tf_op jit(solution)/shard_map/ppermute | solution.py:413
  6.2 22.4 %collective-permute-start.1 = (bf16[256,768]{1,0:T(8,128)(2,1)}, bf16[256,768]{1,0:T(8,128)(2,1)S(1)}, u32[]{:S(2)}, u32[]{:S(2)}) collective-permute-start(bf16[256,768]{1,0:T(8,128)(2,1)} %get-tuple-element.34.refs_0_), channel_id=1, source_target_pairs={{0,4},{1,5},{2,6},{3,7},{4,8},{5,9},{6,10},{7,11},{8,12},{9,13},{1... | collective-permute-start | bytes 1179656 | tf_op jit(solution)/shard_map/ppermute | solution.py:413
  7.5 21.1 %collective-permute-start.2 = (bf16[256,768]{1,0:T(8,128)(2,1)}, bf16[256,768]{1,0:T(8,128)(2,1)S(1)}, u32[]{:S(2)}, u32[]{:S(2)}) collective-permute-start(bf16[256,768]{1,0:T(8,128)(2,1)} %get-tuple-element.34.refs_0_), channel_id=1, source_target_pairs={{0,12},{1,13},{2,14},{3,15},{4,0},{5,1},{6,2},{7,3},{8,4},{9,5},{1... | collective-permute-start | bytes 1179656 | tf_op jit(solution)/shard_map/ppermute | solution.py:413
  9.0 21.8 %collective-permute-start.7 = (bf16[256,768]{1,0:T(8,128)(2,1)}, bf16[256,768]{1,0:T(8,128)(2,1)S(1)}, u32[]{:S(2)}, u32[]{:S(2)}) collective-permute-start(bf16[256,768]{1,0:T(8,128)(2,1)} %get-tuple-element.32), channel_id=1, source_target_pairs={{0,1},{1,2},{2,3},{3,4},{4,5},{5,6},{6,7},{7,8},{8,9},{9,10},{10,1... | collective-permute-start | bytes 1179656 | tf_op jit(solution)/shard_map/ppermute | solution.py:413
  12.0 19.1 %collective-permute-start.8 = (bf16[256,768]{1,0:T(8,128)(2,1)}, bf16[256,768]{1,0:T(8,128)(2,1)S(1)}, u32[]{:S(2)}, u32[]{:S(2)}) collective-permute-start(bf16[256,768]{1,0:T(8,128)(2,1)} %get-tuple-element.33), channel_id=1, source_target_pairs={{1,0},{2,1},{3,2},{4,3},{5,4},{6,5},{7,6},{8,7},{9,8},{10,9},{11,1... | collective-permute-start | bytes 1179656 | tf_op jit(solution)/shard_map/ppermute | solution.py:413
  15.3 1.4 %copy-start = (bf16[1024,768]{1,0:T(8,128)(2,1)S(1)}, bf16[1024,768]{1,0:T(8,128)(2,1)}, u32[]{:S(2)}) copy-start(bf16[1024,768]{1,0:T(8,128)(2,1)} %points_ref) | copy-start | bytes 4718596
  16.7 2.0 %copy-start.1 = (bf16[768,2304]{1,0:T(8,128)(2,1)S(1)}, bf16[768,2304]{1,0:T(8,128)(2,1)}, u32[]{:S(2)}) copy-start(bf16[768,2304]{1,0:T(8,128)(2,1)} %wv_ref.1) | copy-start | bytes 10616836
  18.7 1.3 copy-start.4
  20.0 6.5 %copy-start.5 = (bf16[256,768]{1,0:T(8,128)(2,1)S(1)}, bf16[256,768]{1,0:T(8,128)(2,1)}, u32[]{:S(2)}) copy-start(bf16[256,768]{1,0:T(8,128)(2,1)} %get-tuple-element.34.refs_0_) | copy-start | bytes 1179652
  20.0 11.2 %copy-start.2 = (bf16[768,2304]{1,0:T(8,128)(2,1)S(1)}, bf16[768,2304]{1,0:T(8,128)(2,1)}, u32[]{:S(2)}) copy-start(bf16[768,2304]{1,0:T(8,128)(2,1)} %wv_ref.1) | copy-start | bytes 10616836
  20.0 11.2 %copy-start.6 = (s32[8,8]{1,0:T(8,128)S(1)}, s32[8,8]{1,0:T(8,128)}, u32[]{:S(2)}) copy-start(s32[8,8]{1,0:T(8,128)} %ids_ref.1) | copy-start | bytes 772
  20.0 11.2 %copy-start.7 = (s32[8]{0:T(128)S(1)}, s32[8]{0:T(128)}, u32[]{:S(2)}) copy-start(s32[8]{0:T(128)} %count_ref.1) | copy-start | bytes 100
  26.5 18.1 %copy-start.8 = (bf16[1024,3072]{1,0:T(8,128)(2,1)}, bf16[1024,3072]{1,0:T(8,128)(2,1)S(1)}, u32[]{:S(2)}) copy-start(bf16[1024,3072]{1,0:T(8,128)(2,1)S(1)} %shard_map.119.queries_ref.projected_ref) | copy-start | bytes 18874372
  26.5 20.5 %copy-start.3 = (bf16[768,1536]{1,0:T(8,128)(2,1)S(1)}, bf16[768,1536]{1,0:T(8,128)(2,1)}, u32[]{:S(2)}) copy-start(bf16[768,1536]{1,0:T(8,128)(2,1)} %refs_9_.1) | copy-start | bytes 7077892
  26.5 18.1 %collective-permute-start.3 = (bf16[256,768]{1,0:T(8,128)(2,1)S(1)}, bf16[256,768]{1,0:T(8,128)(2,1)S(1)}, u32[]{:S(2)}, u32[]{:S(2)}) collective-permute-start(bf16[256,768]{1,0:T(8,128)(2,1)S(1)} %copy-done.5), channel_id=1, source_target_pairs={{0,8},{1,9},{2,10},{3,11},{4,12},{5,13},{6,14},{7,15},{8,0},{9,1},... | collective-permute-start | bytes 1179656 | tf_op jit(solution)/shard_map/ppermute | solution.py:413
  28.6 16.0 %collective-permute-start.4 = (bf16[256,768]{1,0:T(8,128)(2,1)S(1)}, bf16[256,768]{1,0:T(8,128)(2,1)S(1)}, u32[]{:S(2)}, u32[]{:S(2)}) collective-permute-start(bf16[256,768]{1,0:T(8,128)(2,1)S(1)} %collective-permute-done.1.refs_2_), channel_id=1, source_target_pairs={{0,2},{1,3},{2,0},{3,1},{4,6},{5,7},{6,4},{7,5},{8,10},{9,11},{10,... | collective-permute-start | bytes 1179656 | tf_op jit(solution)/shard_map/ppermute | solution.py:413
  30.7 16.3 %collective-permute-start.5 = (bf16[256,768]{1,0:T(8,128)(2,1)S(1)}, bf16[256,768]{1,0:T(8,128)(2,1)S(1)}, u32[]{:S(2)}, u32[]{:S(2)}) collective-permute-start(bf16[256,768]{1,0:T(8,128)(2,1)S(1)} %collective-permute-done.2.refs_3_), channel_id=1, source_target_pairs={{0,2},{1,3},{2,0},{3,1},{4,6},{5,7},{6,4},{7,5},{8,10},{9,11},{10,... | collective-permute-start | bytes 1179656 | tf_op jit(solution)/shard_map/ppermute | solution.py:413
  30.8 16.2 %collective-permute-start.6 = (bf16[256,768]{1,0:T(8,128)(2,1)S(1)}, bf16[256,768]{1,0:T(8,128)(2,1)S(1)}, u32[]{:S(2)}, u32[]{:S(2)}) collective-permute-start(bf16[256,768]{1,0:T(8,128)(2,1)S(1)} %collective-permute-done.refs_1_), channel_id=1, source_target_pairs={{0,8},{1,9},{2,10},{3,11},{4,12},{5,13},{6,14},{7,15},{8,0},{9,1},... | collective-permute-start | bytes 1179656 | tf_op jit(solution)/shard_map/ppermute | solution.py:413
  44.6 10.0 %copy-start.9 = (bf16[1024,768]{1,0:T(8,128)(2,1)}, bf16[1024,768]{1,0:T(8,128)(2,1)S(1)}, u32[]{:S(2)}) copy-start(bf16[1024,768]{1,0:T(8,128)(2,1)S(1)} %shard_map.120.block_ref) | copy-start | bytes 4718596
  54.6 36.3 %collective-permute-start.9 = (bf16[2048,1536]{1,0:T(8,128)(2,1)}, bf16[2048,1536]{1,0:T(8,128)(2,1)}, u32[]{:S(2)}, u32[]{:S(2)}) collective-permute-start(bf16[2048,1536]{1,0:T(8,128)(2,1)} %shard_map.121.keys_ref.values_ref), channel_id=1, source_target_pairs={{0,1},{1,0},{2,3},{3,2},{4,5},{5,4},{6,7},{7,6},{8,9},{9,8},{10,11... | collective-permute-start | bytes 18874376 | tf_op jit(solution)/shard_map/ppermute | solution.py:413
